TPU v7x, 256 devices: a whole 4x4x8 slice. The times are simulated.
256 devices in a mesh: seq: 64 (over x, y, z_lo, core), chan: 4 (over z_hi).
Axes of the slice: x: 4, y: 4, z: 8 (z_hi: 4, z_lo: 2; z = z_hi * 2 + z_lo), core: 2. Of those that a mesh axis runs over, the one named last changes fastest.
Arguments:
- query_stream: bfloat16 [16384, 4096], P('seq', 'chan'), may hold values from -6 to 6
- key_stream: bfloat16 [16384, 4096], P('seq', 'chan'), may hold values from -6 to 6
- value_stream: bfloat16 [16384, 4096], P('seq', 'chan'), may hold values from -6 to 6
- filters: bfloat16 [256, 16384], P('chan', 'seq'), may hold values from -0.046875 to 0.046875
- out_weight: bfloat16 [4096, 4096], P('chan'), may hold values from -0.125 to 0.125
- cotangent: bfloat16 [16384, 4096], P('seq', 'chan'), may hold values from -6 to 6
Outputs:
- output: bfloat16 [16384, 4096], P('seq', 'chan')
- query_grad: bfloat16 [16384, 4096], P('seq', 'chan')
- key_grad: bfloat16 [16384, 4096], P('seq', 'chan')
- value_grad: bfloat16 [16384, 4096], P('seq', 'chan')
All inputs are finite; a program needn't handle non-finite values.
Results may differ from a plain program's by a relative error of at most 0.015.
Values may be sent and summed in bfloat16 or wider, within the bound.
A program may use at most 64 MiB of HBM per device.

v0:
```python
import functools

import jax
import jax.numpy as jnp
from jax import lax
from jax.experimental import pallas as pl
from jax.experimental.pallas import tpu as pltpu
from jax.sharding import PartitionSpec as P

MESH = pl.DeviceIdType.MESH
f32, bf16 = jnp.float32, jnp.bfloat16
TOK = 256
WID = 1024
SEQ = 64
CHAN = 4
SUB = 16
PAD = 16
HALF = TOK // 2
CH = 128
NCH = WID // CH


def build_toeplitz(filt, toep):
    row = lax.broadcasted_iota(jnp.int32, (CH, CH), 0)
    col = lax.broadcasted_iota(jnp.int32, (CH, CH), 1)
    keep = col >= row

    def skew(k, half):
        line = filt[k, pl.ds(half, 1), :]
        return pltpu.roll(jnp.broadcast_to(line, (CH, CH)), 0, 1, stride=1, stride_axis=0)

    def step(k, carry):
        last_roll, last = carry
        first_roll = skew(k, 0)
        first = jnp.where(keep, first_roll, last_roll).astype(bf16)
        second_roll = skew(k, 1)
        second = jnp.where(keep, second_roll, first_roll).astype(bf16)
        toep[k, 0:CH, 0:CH] = first
        toep[k, 0:CH, CH:TOK] = second
        toep[k, CH:TOK, 0:CH] = last
        toep[k, CH:TOK, CH:TOK] = first
        return second_roll, second

    zero = jnp.zeros((CH, CH), f32)
    lax.fori_loop(0, SEQ, step, (zero, zero.astype(bf16)))


def conv_blocks(x, toep, acc, adjoint):
    unit = 4
    for group in range(4):
        blocks = SEQ - 16 * group
        rows = blocks * SUB

        def step(m, _, group=group, blocks=blocks, rows=rows):
            k = 16 * group + m * unit
            if adjoint:
                part = sum(
                    lax.dot_general(
                        x[pl.ds(k + u, blocks)].reshape(rows, TOK),
                        toep[k + u],
                        (((1,), (1,)), ((), ())),
                        preferred_element_type=f32,
                    )
                    for u in range(unit)
                )
                at = pl.ds(0, rows)
            else:
                left = jnp.concatenate(
                    [
                        x[pl.ds(PAD + 16 * group - k - u, blocks)].reshape(rows, TOK)
                        for u in range(unit)
                    ],
                    axis=1,
                )
                right = toep[pl.ds(k, unit)].reshape(unit * TOK, TOK)
                part = jnp.dot(left, right, preferred_element_type=f32)
                at = pl.ds(TOK * group, rows)
            if group == 0:

                @pl.when(m == 0)
                def _():
                    acc[at] = part

                @pl.when(m > 0)
                def _():
                    acc[at] += part

            else:
                acc[at] += part
            return 0

        lax.fori_loop(0, 16 // unit, step, 0)


def kernel(
    q_hbm, k_hbm, v_hbm, f_hbm, w_hbm, c_hbm,
    out_hbm, qg_hbm, kg_hbm, vg_hbm,
    q, k, v, cot, f_own, w, f_all, toep,
    send_a, seq_x, seq_y, conv_t, q_t, gated, acc,
    send_g, seq_g, seq_z, gm_t, gg, cots,
    p_far, p_right, p_left, p_own, from_r1, from_l1, from_r2, from_l2, sum_r, sum_l,
    o_out, o_qg, o_kg, o_vg,
    load_sem, w_sem, store_sem, a2a_send, a2a_recv, ag_send, ag_recv, rs_send, rs_recv,
):
    s, c = lax.axis_index("seq"), lax.axis_index("chan")
    right, left, far = (lax.rem(c + d, CHAN) for d in (1, 3, 2))

    loads = [
        pltpu.make_async_copy(src, dst, load_sem.at[i])
        for i, (src, dst) in enumerate(
            ((k_hbm, k), (v_hbm, v), (f_hbm, f_own), (c_hbm, cot), (q_hbm, q))
        )
    ]
    for copy in loads:
        copy.start()
    w_loads = [
        pltpu.make_async_copy(w_hbm.at[:, pl.ds(o * WID, WID)], w.at[o], w_sem.at[o])
        for o in range(CHAN)
    ]
    for copy in w_loads:
        copy.start()

    barrier = pltpu.get_barrier_semaphore()

    def greet(d, _):
        pl.semaphore_signal(barrier, inc=1, device_id=(lax.rem(s + d, SEQ), c), device_id_type=MESH)
        return 0

    lax.fori_loop(1, SEQ, greet, 0)
    for other in (right, left, far):
        pl.semaphore_signal(barrier, inc=1, device_id=(s, other), device_id_type=MESH)

    def exchange(src, dst, offset, which):
        def step(d, _):
            to = lax.rem(s + d, SEQ)
            pltpu.make_async_remote_copy(
                src_ref=src.at[to],
                dst_ref=dst.at[offset + s],
                send_sem=a2a_send.at[which],
                recv_sem=a2a_recv.at[which],
                device_id=(to, c),
                device_id_type=MESH,
            ).start()
            return 0

        lax.fori_loop(1, SEQ, step, 0)

    def received(dst, which):
        part = dst.at[pl.ds(0, SEQ - 1)]
        pltpu.make_async_copy(part, part, a2a_recv.at[which]).wait()

    def sent(src, which):
        part = src.at[pl.ds(0, SEQ - 1)]
        pltpu.make_async_copy(part, part, a2a_send.at[which]).wait()

    def chan_copy(src, dst, to, send, recv):
        return pltpu.make_async_remote_copy(
            src_ref=src,
            dst_ref=dst,
            send_sem=send,
            recv_sem=recv,
            device_id=(s, to),
            device_id_type=MESH,
        )

    loads[0].wait()
    loads[1].wait()

    def mix(j, _):
        at = pl.ds(pl.multiple_of(j * CH, CH), CH)
        mixed = (k[:, at].astype(f32) * v[:, at].astype(f32)).astype(bf16)
        turned = mixed.astype(f32).T.astype(bf16)
        send_a[pl.ds(j * (CH // SUB), CH // SUB)] = turned.reshape(CH // SUB, SUB, TOK)
        return 0

    lax.fori_loop(0, NCH, mix, 0)
    loads[2].wait()
    loads[3].wait()
    pl.semaphore_wait(barrier, SEQ + CHAN - 2)

    low, high = pl.ds(0, HALF), pl.ds(HALF, HALF)
    first_r = chan_copy(cot.at[low], cots.at[c, low], right, ag_send.at[0], ag_recv.at[0])
    first_l = chan_copy(cot.at[high], cots.at[c, high], left, ag_send.at[1], ag_recv.at[1])
    second_r = chan_copy(cot.at[high], cots.at[c, high], right, ag_send.at[2], ag_recv.at[2])
    second_l = chan_copy(cot.at[low], cots.at[c, low], left, ag_send.at[3], ag_recv.at[3])
    on_r = chan_copy(cots.at[left, low], cots.at[left, low], right, ag_send.at[4], ag_recv.at[4])
    on_l = chan_copy(cots.at[right, high], cots.at[right, high], left, ag_send.at[5], ag_recv.at[5])
    first_r.start()
    first_l.start()
    exchange(f_own, f_all, 0, 0)
    exchange(send_a, seq_x, PAD, 1)
    second_r.start()
    second_l.start()
    f_all[s] = f_own[s]
    seq_x[PAD + s] = send_a[s]
    seq_x[0:PAD] = jnp.zeros((PAD, SUB, TOK), bf16)
    seq_g[SEQ : SEQ + PAD] = jnp.zeros((PAD, SUB, TOK), bf16)

    loads[4].wait()

    def turn_q(j, _):
        at = pl.ds(pl.multiple_of(j * CH, CH), CH)
        q_t[pl.ds(pl.multiple_of(j * CH, CH), CH), :] = q[:, at].astype(f32).T.astype(bf16)
        return 0

    lax.fori_loop(0, NCH, turn_q, 0)

    received(f_all, 0)
    build_toeplitz(f_all, toep)

    first_r.wait_recv()
    on_r.start()
    first_l.wait_recv()
    on_l.start()

    received(seq_x, 1)
    conv_blocks(seq_x, toep, acc, False)

    def round_into(dst, j):
        rows = pl.ds(pl.multiple_of(j * CH, CH), CH)
        dst[pl.ds(j * (CH // SUB), CH // SUB)] = (
            acc[rows, :].astype(bf16).reshape(CH // SUB, SUB, TOK)
        )
        return 0

    lax.fori_loop(0, NCH, lambda j, _: round_into(seq_y, j), 0)
    exchange(seq_y, conv_t, 0, 2)
    conv_t[s] = seq_y[s]

    for copy in w_loads:
        copy.wait()

    def grad_part(owner, block, start):
        def step(j, _):
            rows = pl.ds(pl.multiple_of(j * TOK, TOK), TOK)
            part = lax.dot_general(
                w[owner, rows, :], block[...], (((1,), (1,)), ((), ())), preferred_element_type=f32
            )
            if start:
                gg[rows, :] = part
            else:
                gg[rows, :] += part
            return 0

        lax.fori_loop(0, WID // TOK, step, 0)

    grad_part(c, cot, True)
    second_r.wait_recv()
    grad_part(left, cots.at[left], False)
    second_l.wait_recv()
    grad_part(right, cots.at[right], False)

    received(conv_t, 2)

    def gate(j, _):
        at = pl.ds(pl.multiple_of(j * CH, CH), CH)
        conv = conv_t[pl.ds(j * (CH // SUB), CH // SUB)].reshape(CH, TOK)
        turned = (q_t[at, :].astype(f32) * conv.astype(f32)).astype(bf16)
        gated[:, at] = turned.astype(f32).T.astype(bf16)
        return 0

    lax.fori_loop(0, NCH, gate, 0)

    def output_part(owner, dst, keep=None, keep_rows=None):
        def step(j, _):
            at = pl.ds(pl.multiple_of(j * TOK, TOK), TOK)
            part = jnp.dot(gated[...], w[owner, :, at], preferred_element_type=f32)
            dst[:, at] = part.astype(dst.dtype)
            if keep is not None:
                keep[:, at] = part[keep_rows]
            return 0

        lax.fori_loop(0, WID // TOK, step, 0)

    output_part(far, p_far)
    far_r = chan_copy(p_far.at[low], from_l1, right, rs_send.at[0], rs_recv.at[0])
    far_l = chan_copy(p_far.at[high], from_r1, left, rs_send.at[1], rs_recv.at[1])
    far_r.start()
    far_l.start()
    output_part(right, p_right, sum_r, slice(0, HALF))
    near_r = chan_copy(p_right.at[high], from_l2.at[high], right, rs_send.at[2], rs_recv.at[2])
    near_r.start()
    output_part(left, p_left, sum_l, slice(HALF, TOK))
    near_l = chan_copy(p_left.at[low], from_r2.at[low], left, rs_send.at[3], rs_recv.at[3])
    near_l.start()

    on_r.wait_recv()
    on_l.wait_recv()
    grad_part(far, cots.at[far], False)

    def to_grad_conv(j, _):
        at = pl.ds(pl.multiple_of(j * CH, CH), CH)
        rounded = gg[at, :].astype(bf16).astype(f32)
        grad_conv = (rounded * q_t[at, :].astype(f32)).astype(bf16)
        send_g[pl.ds(j * (CH // SUB), CH // SUB)] = grad_conv.reshape(CH // SUB, SUB, TOK)
        return 0

    lax.fori_loop(0, NCH, to_grad_conv, 0)
    exchange(send_g, seq_g, 0, 3)
    seq_g[s] = send_g[s]

    output_part(c, p_own)

    def to_query_grad(j, _):
        at = pl.ds(pl.multiple_of(j * CH, CH), CH)
        conv = conv_t[pl.ds(j * (CH // SUB), CH // SUB)].reshape(CH, TOK)
        turned = gg[at, :].astype(bf16).astype(f32) * conv.astype(f32)
        o_qg[:, at] = turned.T.astype(bf16)
        return 0

    lax.fori_loop(0, NCH, to_query_grad, 0)
    store_qg = pltpu.make_async_copy(o_qg, qg_hbm, store_sem.at[0])
    store_qg.start()

    far_r.wait_recv()
    p_right[low, :] = (sum_r[...] + from_l1[...].astype(f32)).astype(bf16)
    pass_r = chan_copy(p_right.at[low], from_l2.at[low], right, rs_send.at[4], rs_recv.at[4])
    pass_r.start()
    far_l.wait_recv()
    p_left[high, :] = (sum_l[...] + from_r1[...].astype(f32)).astype(bf16)
    pass_l = chan_copy(p_left.at[high], from_r2.at[high], left, rs_send.at[5], rs_recv.at[5])
    pass_l.start()

    received(seq_g, 3)
    conv_blocks(seq_g, toep, acc, True)
    lax.fori_loop(0, NCH, lambda j, _: round_into(seq_z, j), 0)
    exchange(seq_z, gm_t, 0, 4)
    gm_t[s] = seq_z[s]

    near_r.wait_recv()
    near_l.wait_recv()
    pass_r.wait_recv()
    pass_l.wait_recv()

    def to_output(j, _):
        at = pl.ds(pl.multiple_of(j * CH, CH), CH)
        o_out[:, at] = (
            p_own[:, at] + from_l2[:, at].astype(f32) + from_r2[:, at].astype(f32)
        ).astype(bf16)
        return 0

    lax.fori_loop(0, NCH, to_output, 0)
    store_out = pltpu.make_async_copy(o_out, out_hbm, store_sem.at[1])
    store_out.start()

    received(gm_t, 4)

    def to_grads(j, _):
        at = pl.ds(pl.multiple_of(j * CH, CH), CH)
        grad = gm_t[pl.ds(j * (CH // SUB), CH // SUB)].reshape(CH, TOK).astype(f32).T
        o_kg[:, at] = (grad * v[:, at].astype(f32)).astype(bf16)
        o_vg[:, at] = (grad * k[:, at].astype(f32)).astype(bf16)
        return 0

    lax.fori_loop(0, NCH, to_grads, 0)
    store_kg = pltpu.make_async_copy(o_kg, kg_hbm, store_sem.at[2])
    store_vg = pltpu.make_async_copy(o_vg, vg_hbm, store_sem.at[3])
    store_kg.start()
    store_vg.start()

    sent(f_own, 0)
    for which, src in ((1, send_a), (2, seq_y), (3, send_g), (4, seq_z)):
        sent(src, which)
    for copy in (first_r, first_l, second_r, second_l, on_r, on_l):
        copy.wait_send()
    for copy in (far_r, far_l, near_r, near_l, pass_r, pass_l):
        copy.wait_send()
    for copy in (store_qg, store_out, store_kg, store_vg):
        copy.wait()


def local(query, key, value, filters, weight, cotangent):
    lines = filters.astype(f32).reshape(SEQ, 2, CH)
    stream = jax.ShapeDtypeStruct((TOK, WID), bf16)
    here = pl.BlockSpec(memory_space=pl.ANY)
    rows = pltpu.VMEM((TOK, WID), bf16)
    turned = pltpu.VMEM((SEQ, SUB, TOK), bf16)
    padded = pltpu.VMEM((SEQ + PAD, SUB, TOK), bf16)
    lines_at = pltpu.VMEM((SEQ, 2, CH), f32)
    half = pltpu.VMEM((HALF, WID), bf16)
    half_sum = pltpu.VMEM((HALF, WID), f32)
    dma = pltpu.SemaphoreType.DMA
    return pl.pallas_call(
        kernel,
        out_shape=(stream,) * 4,
        in_specs=[here] * 6,
        out_specs=(here,) * 4,
        scratch_shapes=[
            rows, rows, rows, rows,
            lines_at,
            pltpu.VMEM((CHAN, WID, WID), bf16),
            lines_at,
            pltpu.VMEM((SEQ, TOK, TOK), bf16),
            turned, padded, turned, turned,
            pltpu.VMEM((WID, TOK), bf16),
            rows,
            pltpu.VMEM((WID, TOK), f32),
            turned, padded, turned, turned,
            pltpu.VMEM((WID, TOK), f32),
            pltpu.VMEM((CHAN, TOK, WID), bf16),
            rows, rows, rows,
            pltpu.VMEM((TOK, WID), f32),
            half, half, rows, rows,
            half_sum, half_sum,
            rows, rows, rows, rows,
            dma((5,)), dma((CHAN,)), dma((4,)), dma((5,)), dma((5,)),
            dma((6,)), dma((6,)), dma((6,)), dma((6,)),
        ],
        compiler_params=pltpu.CompilerParams(
            collective_id=0, has_side_effects=True, vmem_limit_bytes=56 << 20
        ),
        cost_estimate=pl.CostEstimate(
            flops=18_000_000_000, bytes_accessed=12 << 20, transcendentals=0
        ),
    )(query, key, value, lines, weight, cotangent)


def solution(mesh):
    split = P("seq", "chan")
    return jax.shard_map(
        local,
        mesh=mesh,
        in_specs=(split, split, split, P("chan", "seq"), P("chan", None), split),
        out_specs=(split,) * 4,
        check_vma=False,
    )
```

profile of v0, /device:TPU:1, one launch (start us, length us, event | category | flops | bytes accessed | tf_op | source)
XLA Modules:
  0.0 130.6 jit_solution(14432630007622770046)
XLA Ops:
  0.6 1.4 %reshape.16.f_hbm = f32[64,2,128]{2,1,0:T(2,128)} reshape(bf16[64,256]{1,0:T(8,128)(2,1)} %param.9) | data formatting | bytes 98304 | tf_op jit(solution)/shard_map/reshape | solution.py:373
  2.1 121.0 %shard_map.93 = (bf16[256,1024]{1,0:T(8,128)(2,1)}, bf16[256,1024]{1,0:T(8,128)(2,1)}, bf16[256,1024]{1,0:T(8,128)(2,1)}, bf16[256,1024]{1,0:T(8,128)(2,1)}) custom-call(bf16[256,1024]{1,0:T(8,128)(2,1)} %q_hbm.1, bf16[256,1024]{1,0:T(8,128)(2,1)} %k_hbm.1, bf16[256,1024]{1,0:T(8,128)(2,1)} %v_hbm.1, f32[64,2,128]{2,1,0:T(2,128)} %reshape.16.f_hbm, ...), custom_call_target="tpu_custom_call" | custom-call | flops 17999998976 | bytes 12582912 | tf_op jit(solution)/shard_map/pallas_call | solution.py:383
  123.1 1.9 %copy.14 = bf16[256,1024]{1,0:T(8,128)(2,1)} copy(bf16[256,1024]{1,0:T(8,128)(2,1)} %get-tuple-element.8) | data formatting | bytes 1048576
  125.0 1.9 %copy.15 = bf16[256,1024]{1,0:T(8,128)(2,1)} copy(bf16[256,1024]{1,0:T(8,128)(2,1)} %get-tuple-element.9) | data formatting | bytes 1048576
  126.8 1.9 %copy.16 = bf16[256,1024]{1,0:T(8,128)(2,1)} copy(bf16[256,1024]{1,0:T(8,128)(2,1)} %get-tuple-element.10) | data formatting | bytes 1048576
  128.7 1.9 %copy.17 = bf16[256,1024]{1,0:T(8,128)(2,1)} copy(bf16[256,1024]{1,0:T(8,128)(2,1)} %get-tuple-element.11) | data formatting | bytes 1048576
where the time goes:
time: 131 us
  Pallas kernels  121 us (92%)
  local copies, waits for them, and re-layouts  8.89 us (7%)
    pallas_call x1, Pallas kernels, local(): pl.pallas_call(kernel, out_shape=(stream,) * 4, in_specs=[here] * 6, out_...  121 us
    unnamed x4, local copies, waits for them, and re-layouts  7.47 us

commit v1 on v0

v1 whole, which is shorter than its diff:
```python
import functools

import jax
import jax.numpy as jnp
from jax import lax
from jax.experimental import pallas as pl
from jax.experimental.pallas import tpu as pltpu
from jax.sharding import PartitionSpec as P

MESH = pl.DeviceIdType.MESH
f32, bf16 = jnp.float32, jnp.bfloat16
TOK = 256
WID = 1024
SEQ = 64
CHAN = 4
SUB = 16
PAD = 16
HALF = TOK // 2
CH = 128
NCH = WID // CH
PART = 16
PARTS = SEQ // PART
ROW = CH // SUB


def build_toeplitz(filt, toep):
    row = lax.broadcasted_iota(jnp.int32, (CH, CH), 0)
    col = lax.broadcasted_iota(jnp.int32, (CH, CH), 1)
    keep = col >= row

    def skew(k, half):
        line = filt[k, pl.ds(half, 1), :]
        return pltpu.roll(jnp.broadcast_to(line, (CH, CH)), 0, 1, stride=1, stride_axis=0)

    def step(k, carry):
        last_roll, last = carry
        first_roll = skew(k, 0)
        first = jnp.where(keep, first_roll, last_roll).astype(bf16)
        second_roll = skew(k, 1)
        second = jnp.where(keep, second_roll, first_roll).astype(bf16)
        toep[k, 0:CH, 0:CH] = first
        toep[k, 0:CH, CH:TOK] = second
        toep[k, CH:TOK, 0:CH] = last
        toep[k, CH:TOK, CH:TOK] = first
        return second_roll, second

    zero = jnp.zeros((CH, CH), f32)
    lax.fori_loop(0, SEQ, step, (zero, zero.astype(bf16)))


def conv_chunk(x, toep, acc, chunk, adjoint):
    unit = 8

    def step(m, _):
        k = m * unit
        first = PART * chunk + k if adjoint else PAD + PART * chunk - k
        sign = 1 if adjoint else -1
        left = jnp.concatenate(
            [x[pl.ds(first + sign * u, PART)].reshape(PART * SUB, TOK) for u in range(unit)], axis=1
        )
        if adjoint:
            right = jnp.concatenate([toep[k + u] for u in range(unit)], axis=1)
            part = lax.dot_general(
                left, right, (((1,), (1,)), ((), ())), preferred_element_type=f32
            )
        else:
            right = toep[pl.ds(k, unit)].reshape(unit * TOK, TOK)
            part = jnp.dot(left, right, preferred_element_type=f32)
        acc[...] += part
        return 0

    acc[...] = jnp.zeros_like(acc)
    steps = PART // unit
    lax.fori_loop(0, (PARTS - chunk) * steps if adjoint else (chunk + 1) * steps, step, 0)


def kernel(
    q_hbm, k_hbm, v_hbm, f_hbm, w_hbm, c_hbm,
    gm_t, qg_hbm, own_hbm, from_r2, from_l2,
    q, k, v, cot, f_raw, f_own, w, f_all, toep,
    send_a, seq_x, seq_y, conv_t, q_t, gated, acc,
    send_g, seq_g, seq_z, gg, cots,
    p_far, p_right, p_left, p_own, from_r1, from_l1, sum_r, sum_l, o_qg,
    load_sem, w_sem, store_sem, a2a_send, a2a_recv, ag_send, ag_recv, rs_send, rs_recv,
):
    s, c = lax.axis_index("seq"), lax.axis_index("chan")
    right, left, far = (lax.rem(c + d, CHAN) for d in (1, 3, 2))

    loads = [
        pltpu.make_async_copy(src, dst, load_sem.at[i])
        for i, (src, dst) in enumerate(
            ((k_hbm, k), (v_hbm, v), (f_hbm, f_raw), (c_hbm, cot), (q_hbm, q))
        )
    ]
    for copy in loads:
        copy.start()
    w_loads = [
        pltpu.make_async_copy(w_hbm.at[:, pl.ds(o * WID, WID)], w.at[o], w_sem.at[o])
        for o in range(CHAN)
    ]
    for copy in w_loads:
        copy.start()

    barrier = pltpu.get_barrier_semaphore()

    def greet(d, _):
        pl.semaphore_signal(barrier, inc=1, device_id=(lax.rem(s + d, SEQ), c), device_id_type=MESH)
        return 0

    lax.fori_loop(1, SEQ, greet, 0)
    for other in (right, left, far):
        pl.semaphore_signal(barrier, inc=1, device_id=(s, other), device_id_type=MESH)

    def send_block(src, dst, offset, which, to):
        @pl.when(to != s)
        def _():
            pltpu.make_async_remote_copy(
                src_ref=src.at[to],
                dst_ref=dst.at[offset + s],
                send_sem=a2a_send.at[which],
                recv_sem=a2a_recv.at[which],
                device_id=(to, c),
                device_id_type=MESH,
            ).start()

    def send_blocks(src, dst, offset, which, first, count):
        def step(d, _):
            send_block(src, dst, offset, which, first + lax.rem(lax.rem(s, count) + d, count))
            return 0

        lax.fori_loop(0, count, step, 0)

    def convolve(x, out, dst, which, adjoint):
        def step(i, _):
            chunk = lax.rem(s // PART + i, PARTS)
            conv_chunk(x, toep, acc, chunk, adjoint)
            at = pl.multiple_of(chunk * PART, PART)
            out[pl.ds(at, PART)] = acc[...].astype(bf16).reshape(PART, SUB, TOK)
            send_blocks(out, dst, 0, which, chunk * PART, PART)
            return 0

        lax.fori_loop(0, PARTS, step, 0)

    def received(dst, which):
        part = dst.at[pl.ds(0, SEQ - 1)]
        pltpu.make_async_copy(part, part, a2a_recv.at[which]).wait()

    def sent(src, which):
        part = src.at[pl.ds(0, SEQ - 1)]
        pltpu.make_async_copy(part, part, a2a_send.at[which]).wait()

    def chan_copy(src, dst, to, send, recv):
        return pltpu.make_async_remote_copy(
            src_ref=src,
            dst_ref=dst,
            send_sem=send,
            recv_sem=recv,
            device_id=(s, to),
            device_id_type=MESH,
        )

    pl.semaphore_wait(barrier, SEQ + CHAN - 2)

    low, high = pl.ds(0, HALF), pl.ds(HALF, HALF)
    first_r = chan_copy(c_hbm.at[low], cots.at[c, low], right, ag_send.at[0], ag_recv.at[0])
    first_l = chan_copy(c_hbm.at[high], cots.at[c, high], left, ag_send.at[1], ag_recv.at[1])
    second_r = chan_copy(c_hbm.at[high], cots.at[c, high], right, ag_send.at[2], ag_recv.at[2])
    second_l = chan_copy(c_hbm.at[low], cots.at[c, low], left, ag_send.at[3], ag_recv.at[3])
    on_r = chan_copy(cots.at[left, low], cots.at[left, low], right, ag_send.at[4], ag_recv.at[4])
    on_l = chan_copy(cots.at[right, high], cots.at[right, high], left, ag_send.at[5], ag_recv.at[5])
    first_r.start()
    first_l.start()

    loads[2].wait()
    lines = f_raw[...].astype(f32)
    f_own[:, 0, :] = lines[:, 0:CH]
    f_own[:, 1, :] = lines[:, CH:TOK]
    send_blocks(f_own, f_all, 0, 0, 0, SEQ)
    loads[0].wait()
    loads[1].wait()

    def mix(i, _):
        j = lax.rem(s // ROW + i, NCH)
        at = pl.ds(pl.multiple_of(j * CH, CH), CH)
        mixed = (k[:, at].astype(f32) * v[:, at].astype(f32)).astype(bf16)
        turned = mixed.astype(f32).T.astype(bf16)
        send_a[pl.ds(j * ROW, ROW)] = turned.reshape(ROW, SUB, TOK)
        send_blocks(send_a, seq_x, PAD, 1, j * ROW, ROW)
        return 0

    lax.fori_loop(0, NCH, mix, 0)
    second_r.start()
    second_l.start()
    f_all[s] = f_own[s]
    seq_x[PAD + s] = send_a[s]
    seq_x[0:PAD] = jnp.zeros((PAD, SUB, TOK), bf16)
    seq_g[SEQ : SEQ + PAD] = jnp.zeros((PAD, SUB, TOK), bf16)

    loads[4].wait()

    def turn_q(j, _):
        at = pl.ds(pl.multiple_of(j * CH, CH), CH)
        q_t[pl.ds(pl.multiple_of(j * CH, CH), CH), :] = q[:, at].astype(f32).T.astype(bf16)
        return 0

    lax.fori_loop(0, NCH, turn_q, 0)

    received(f_all, 0)
    build_toeplitz(f_all, toep)

    first_r.wait_recv()
    on_r.start()
    first_l.wait_recv()
    on_l.start()

    received(seq_x, 1)
    convolve(seq_x, seq_y, conv_t, 2, False)
    conv_t[s] = seq_y[s]

    loads[3].wait()
    for copy in w_loads:
        copy.wait()

    def grad_part(owner, block, start):
        def step(j, _):
            rows = pl.ds(pl.multiple_of(j * TOK, TOK), TOK)
            part = lax.dot_general(
                w[owner, rows, :], block[...], (((1,), (1,)), ((), ())), preferred_element_type=f32
            )
            if start:
                gg[rows, :] = part
            else:
                gg[rows, :] += part
            return 0

        lax.fori_loop(0, WID // TOK, step, 0)

    grad_part(c, cot, True)
    second_r.wait_recv()
    grad_part(left, cots.at[left], False)
    second_l.wait_recv()
    grad_part(right, cots.at[right], False)
    on_r.wait_recv()
    on_l.wait_recv()
    grad_part(far, cots.at[far], False)

    def to_grad_conv(i, _):
        j = lax.rem(s // ROW + i, NCH)
        at = pl.ds(pl.multiple_of(j * CH, CH), CH)
        rounded = gg[at, :].astype(bf16).astype(f32)
        grad_conv = (rounded * q_t[at, :].astype(f32)).astype(bf16)
        send_g[pl.ds(j * ROW, ROW)] = grad_conv.reshape(ROW, SUB, TOK)
        send_blocks(send_g, seq_g, 0, 3, j * ROW, ROW)
        return 0

    lax.fori_loop(0, NCH, to_grad_conv, 0)
    seq_g[s] = send_g[s]


    received(conv_t, 2)

    def gate(j, _):
        at = pl.ds(pl.multiple_of(j * CH, CH), CH)
        conv = conv_t[pl.ds(j * ROW, ROW)].reshape(CH, TOK)
        turned = (q_t[at, :].astype(f32) * conv.astype(f32)).astype(bf16)
        gated[:, at] = turned.astype(f32).T.astype(bf16)
        return 0

    lax.fori_loop(0, NCH, gate, 0)

    def output_part(owner, dst, keep=None, keep_rows=None):
        def step(j, _):
            at = pl.ds(pl.multiple_of(j * TOK, TOK), TOK)
            part = jnp.dot(gated[...], w[owner, :, at], preferred_element_type=f32)
            dst[:, at] = part.astype(dst.dtype)
            if keep is not None:
                keep[:, at] = part[keep_rows]
            return 0

        lax.fori_loop(0, WID // TOK, step, 0)

    far_r = chan_copy(p_far.at[low], from_l1, right, rs_send.at[0], rs_recv.at[0])
    far_l = chan_copy(p_far.at[high], from_r1, left, rs_send.at[1], rs_recv.at[1])
    near_r = chan_copy(p_right.at[high], from_l2.at[high], right, rs_send.at[2], rs_recv.at[2])
    near_l = chan_copy(p_left.at[low], from_r2.at[low], left, rs_send.at[3], rs_recv.at[3])

    output_part(far, p_far)
    far_r.start()
    far_l.start()
    output_part(right, p_right, sum_r, slice(0, HALF))
    near_r.start()
    output_part(left, p_left, sum_l, slice(HALF, TOK))
    near_l.start()
    output_part(c, p_own)
    store_own = pltpu.make_async_copy(p_own, own_hbm, store_sem.at[1])
    store_own.start()

    def to_query_grad(j, _):
        at = pl.ds(pl.multiple_of(j * CH, CH), CH)
        conv = conv_t[pl.ds(j * ROW, ROW)].reshape(CH, TOK)
        turned = gg[at, :].astype(bf16).astype(f32) * conv.astype(f32)
        o_qg[:, at] = turned.T.astype(bf16)
        return 0

    lax.fori_loop(0, NCH, to_query_grad, 0)
    store_qg = pltpu.make_async_copy(o_qg, qg_hbm, store_sem.at[0])
    store_qg.start()

    received(seq_g, 3)
    convolve(seq_g, seq_z, gm_t, 4, True)
    far_r.wait_recv()
    p_right[low, :] = (sum_r[...] + from_l1[...].astype(f32)).astype(bf16)
    pass_r = chan_copy(p_right.at[low], from_l2.at[low], right, rs_send.at[4], rs_recv.at[4])
    pass_r.start()
    far_l.wait_recv()
    p_left[high, :] = (sum_l[...] + from_r1[...].astype(f32)).astype(bf16)
    pass_l = chan_copy(p_left.at[high], from_r2.at[high], left, rs_send.at[5], rs_recv.at[5])
    pass_l.start()

    own_z = pltpu.make_async_copy(seq_z.at[s], gm_t.at[s], store_sem.at[2])
    own_z.start()

    near_r.wait_recv()
    near_l.wait_recv()
    pass_r.wait_recv()
    pass_l.wait_recv()

    received(gm_t, 4)
    own_z.wait()
    sent(f_own, 0)
    for which, src in ((1, send_a), (2, seq_y), (3, send_g), (4, seq_z)):
        sent(src, which)
    for copy in (first_r, first_l, second_r, second_l, on_r, on_l):
        copy.wait_send()
    for copy in (far_r, far_l, near_r, near_l, pass_r, pass_l):
        copy.wait_send()
    for copy in (store_qg, store_own):
        copy.wait()


def finish_kernel(gm_t, k, v, qg_in, own, from_r, from_l, out, qg, kg, vg):
    width = out.shape[1]
    grad = gm_t[...].reshape(width, TOK).astype(f32).T
    kg[...] = (grad * v[...].astype(f32)).astype(bf16)
    vg[...] = (grad * k[...].astype(f32)).astype(bf16)
    qg[...] = qg_in[...]
    total = own[...].astype(f32) + from_r[...].astype(f32) + from_l[...].astype(f32)
    out[...] = total.astype(bf16)


def local(query, key, value, filters, weight, cotangent):
    stream = jax.ShapeDtypeStruct((TOK, WID), bf16)
    here = pl.BlockSpec(memory_space=pl.ANY)
    rows = pltpu.VMEM((TOK, WID), bf16)
    turned = pltpu.VMEM((SEQ, SUB, TOK), bf16)
    padded = pltpu.VMEM((SEQ + PAD, SUB, TOK), bf16)
    lines_at = pltpu.VMEM((SEQ, 2, CH), f32)
    half = pltpu.VMEM((HALF, WID), bf16)
    half_sum = pltpu.VMEM((HALF, WID), f32)
    dma = pltpu.SemaphoreType.DMA
    gm_t, query_grad, own, from_r, from_l = pl.pallas_call(
        kernel,
        out_shape=(jax.ShapeDtypeStruct((SEQ, SUB, TOK), bf16),) + (stream,) * 4,
        in_specs=[here] * 6,
        out_specs=(here,) * 5,
        scratch_shapes=[
            rows, rows, rows, rows,
            pltpu.VMEM((SEQ, TOK), bf16),
            lines_at,
            pltpu.VMEM((CHAN, WID, WID), bf16),
            lines_at,
            pltpu.VMEM((SEQ, TOK, TOK), bf16),
            turned, padded, turned, turned,
            pltpu.VMEM((WID, TOK), bf16),
            rows,
            pltpu.VMEM((PART * SUB, TOK), f32),
            turned, padded, turned,
            pltpu.VMEM((WID, TOK), f32),
            pltpu.VMEM((CHAN, TOK, WID), bf16),
            rows, rows, rows, rows,
            half, half,
            half_sum, half_sum,
            rows,
            dma((5,)), dma((CHAN,)), dma((3,)), dma((5,)), dma((5,)),
            dma((6,)), dma((6,)), dma((6,)), dma((6,)),
        ],
        compiler_params=pltpu.CompilerParams(
            collective_id=0, has_side_effects=True, vmem_limit_bytes=56 << 20
        ),
        cost_estimate=pl.CostEstimate(
            flops=18_000_000_000, bytes_accessed=12 << 20, transcendentals=0
        ),
    )(query, key, value, filters, weight, cotangent)
    width = 256
    cols = pl.BlockSpec((TOK, width), lambda j: (0, j))
    return pl.pallas_call(
        finish_kernel,
        out_shape=(stream,) * 4,
        grid=(WID // width,),
        in_specs=[pl.BlockSpec((width // SUB, SUB, TOK), lambda j: (j, 0, 0))] + [cols] * 6,
        out_specs=(cols,) * 4,
        cost_estimate=pl.CostEstimate(
            flops=4_000_000, bytes_accessed=6 << 20, transcendentals=0
        ),
    )(gm_t, key, value, query_grad, own, from_r, from_l)


def solution(mesh):
    split = P("seq", "chan")
    return jax.shard_map(
        local,
        mesh=mesh,
        in_specs=(split, split, split, P("chan", "seq"), P("chan", None), split),
        out_specs=(split,) * 4,
        check_vma=False,
    )
```

time: 131 us -> 111 us (0.85)
  Pallas kernels: 121 us -> 110 us
  local copies, waits for them, and re-layouts: 8.89 us -> 0 us
    pallas_call x1 -> x2, Pallas kernels: 121 us -> 110 us  [the longest x1 106 us: local(): pl.pallas_call(kernel, out_shape=(jax.ShapeDtypeStruct((SEQ, SUB, TOK), b...]
    unnamed x4 -> x0, local copies, waits for them, and re-layouts: 7.47 us -> none
    reshape x1 -> x0, local copies, waits for them, and re-layouts: 1.42 us -> none  [local(): lines = filters.astype(f32).reshape(SEQ, 2, CH)]
where the time goes in v1:
time: 111 us
  Pallas kernels  110 us (99%)
    pallas_call x1, Pallas kernels, local(): pl.pallas_call(kernel, out_shape=(jax.ShapeDtypeStruct((SEQ, SUB, TOK), b...  106 us
    pallas_call x1, Pallas kernels, local(): pl.pallas_call(finish_kernel, out_shape=(stream,) * 4, grid=(WID // width...  4.24 us

profile of v1, /device:TPU:1, one launch (start us, length us, event | category | flops | bytes accessed | tf_op | source)
XLA Modules:
  0.0 110.8 jit_solution(9256973861527415661)
XLA Ops:
  0.6 105.9 %shard_map.93 = (bf16[64,16,256]{2,1,0:T(8,128)(2,1)}, bf16[256,1024]{1,0:T(8,128)(2,1)}, bf16[256,1024]{1,0:T(8,128)(2,1)}, bf16[256,1024]{1,0:T(8,128)(2,1)}, bf16[256,1024]{1,0:T(8,128)(2,1)}) custom-call(bf16[256,1024]{1,0:T(8,128)(2,1)} %q_hbm.1, bf16[256,1024]{1,0:T(8,128)(2,1)} %k.1, bf16[256,1024]{1,0:T(8,128)(2,1)} %v.1, bf16[64,256]{1,0:T(8,128)(2,1)} %f_hbm.1, ...), custom_call_target="tpu_custom_call" | custom-call | flops 17999998976 | bytes 12582912 | tf_op jit(solution)/shard_map/pallas_call | solution.py:361
  106.5 4.2 %shard_map.94 = (bf16[256,1024]{1,0:T(8,128)(2,1)}, bf16[256,1024]{1,0:T(8,128)(2,1)}, bf16[256,1024]{1,0:T(8,128)(2,1)}, bf16[256,1024]{1,0:T(8,128)(2,1)}) custom-call(bf16[64,16,256]{2,1,0:T(8,128)(2,1)} %get-tuple-element.9.gm_t, bf16[256,1024]{1,0:T(8,128)(2,1)} %k.1, bf16[256,1024]{1,0:T(8,128)(2,1)} %v.1, bf16[256,1024]{1,0:T(8,128)(2,1)} %get-tuple-element.10.qg_in, ...), custom_call_target="tpu_custom_call" | custom-call | flops 4000000 | bytes 6291456 | tf_op jit(solution)/shard_map/pallas_call | solution.py:396

commit v2 on v1

--- a/solution.py
+++ b/solution.py
@@ -45,7 +45,7 @@
         return second_roll, second
 
     zero = jnp.zeros((CH, CH), f32)
-    lax.fori_loop(0, SEQ, step, (zero, zero.astype(bf16)))
+    lax.fori_loop(0, SEQ, step, (zero, zero.astype(bf16)), unroll=4)
 
 
 def conv_chunk(x, toep, acc, chunk, adjoint):
@@ -188,7 +188,7 @@
         send_blocks(send_a, seq_x, PAD, 1, j * ROW, ROW)
         return 0
 
-    lax.fori_loop(0, NCH, mix, 0)
+    lax.fori_loop(0, NCH, mix, 0, unroll=2)
     second_r.start()
     second_l.start()
     f_all[s] = f_own[s]
@@ -203,7 +203,7 @@
         q_t[pl.ds(pl.multiple_of(j * CH, CH), CH), :] = q[:, at].astype(f32).T.astype(bf16)
         return 0
 
-    lax.fori_loop(0, NCH, turn_q, 0)
+    lax.fori_loop(0, NCH, turn_q, 0, unroll=2)
 
     received(f_all, 0)
     build_toeplitz(f_all, toep)
@@ -233,7 +233,7 @@
                 gg[rows, :] += part
             return 0
 
-        lax.fori_loop(0, WID // TOK, step, 0)
+        lax.fori_loop(0, WID // TOK, step, 0, unroll=2)
 
     grad_part(c, cot, True)
     second_r.wait_recv()
@@ -253,7 +253,7 @@
         send_blocks(send_g, seq_g, 0, 3, j * ROW, ROW)
         return 0
 
-    lax.fori_loop(0, NCH, to_grad_conv, 0)
+    lax.fori_loop(0, NCH, to_grad_conv, 0, unroll=2)
     seq_g[s] = send_g[s]
 
 
@@ -266,7 +266,7 @@
         gated[:, at] = turned.astype(f32).T.astype(bf16)
         return 0
 
-    lax.fori_loop(0, NCH, gate, 0)
+    lax.fori_loop(0, NCH, gate, 0, unroll=2)
 
     def output_part(owner, dst, keep=None, keep_rows=None):
         def step(j, _):
@@ -277,7 +277,7 @@
                 keep[:, at] = part[keep_rows]
             return 0
 
-        lax.fori_loop(0, WID // TOK, step, 0)
+        lax.fori_loop(0, WID // TOK, step, 0, unroll=2)
 
     far_r = chan_copy(p_far.at[low], from_l1, right, rs_send.at[0], rs_recv.at[0])
     far_l = chan_copy(p_far.at[high], from_r1, left, rs_send.at[1], rs_recv.at[1])
@@ -302,7 +302,7 @@
         o_qg[:, at] = turned.T.astype(bf16)
         return 0
 
-    lax.fori_loop(0, NCH, to_query_grad, 0)
+    lax.fori_loop(0, NCH, to_query_grad, 0, unroll=2)
     store_qg = pltpu.make_async_copy(o_qg, qg_hbm, store_sem.at[0])
     store_qg.start()
 
@@ -391,7 +391,7 @@
             flops=18_000_000_000, bytes_accessed=12 << 20, transcendentals=0
         ),
     )(query, key, value, filters, weight, cotangent)
-    width = 256
+    width = 512
     cols = pl.BlockSpec((TOK, width), lambda j: (0, j))
     return pl.pallas_call(
         finish_kernel,

time: 111 us -> 110 us (level)
    pallas_call x1, Pallas kernels: 4.24 us -> 3.1 us  [local(): pl.pallas_call(finish_kernel, out_shape=(stream,) * 4, grid=(WID // width...]
where the time goes in v2:
time: 110 us
  Pallas kernels  109 us (99%)
    pallas_call x1, Pallas kernels, local(): pl.pallas_call(kernel, out_shape=(jax.ShapeDtypeStruct((SEQ, SUB, TOK), b...  106 us
    pallas_call x1, Pallas kernels, local(): pl.pallas_call(finish_kernel, out_shape=(stream,) * 4, grid=(WID // width...  3.1 us

profile of v2, /device:TPU:1, one launch (start us, length us, event | category | flops | bytes accessed | tf_op | source)
XLA Modules:
  0.0 109.6 jit_solution(16468647861215641440)
XLA Ops:
  0.6 105.9 %shard_map.93 = (bf16[64,16,256]{2,1,0:T(8,128)(2,1)}, bf16[256,1024]{1,0:T(8,128)(2,1)}, bf16[256,1024]{1,0:T(8,128)(2,1)}, bf16[256,1024]{1,0:T(8,128)(2,1)}, bf16[256,1024]{1,0:T(8,128)(2,1)}) custom-call(bf16[256,1024]{1,0:T(8,128)(2,1)} %q_hbm.1, bf16[256,1024]{1,0:T(8,128)(2,1)} %k.1, bf16[256,1024]{1,0:T(8,128)(2,1)} %v.1, bf16[64,256]{1,0:T(8,128)(2,1)} %f_hbm.1, ...), custom_call_target="tpu_custom_call" | custom-call | flops 17999998976 | bytes 12582912 | tf_op jit(solution)/shard_map/pallas_call | solution.py:361
  106.5 3.1 %shard_map.94 = (bf16[256,1024]{1,0:T(8,128)(2,1)}, bf16[256,1024]{1,0:T(8,128)(2,1)}, bf16[256,1024]{1,0:T(8,128)(2,1)}, bf16[256,1024]{1,0:T(8,128)(2,1)}) custom-call(bf16[64,16,256]{2,1,0:T(8,128)(2,1)} %get-tuple-element.9.gm_t, bf16[256,1024]{1,0:T(8,128)(2,1)} %k.1, bf16[256,1024]{1,0:T(8,128)(2,1)} %v.1, bf16[256,1024]{1,0:T(8,128)(2,1)} %get-tuple-element.10.qg_in, ...), custom_call_target="tpu_custom_call" | custom-call | flops 4000000 | bytes 6291456 | tf_op jit(solution)/shard_map/pallas_call | solution.py:396

commit v3 on v2

--- a/solution.py
+++ b/solution.py
@@ -168,8 +168,6 @@
     second_l = chan_copy(c_hbm.at[low], cots.at[c, low], left, ag_send.at[3], ag_recv.at[3])
     on_r = chan_copy(cots.at[left, low], cots.at[left, low], right, ag_send.at[4], ag_recv.at[4])
     on_l = chan_copy(cots.at[right, high], cots.at[right, high], left, ag_send.at[5], ag_recv.at[5])
-    first_r.start()
-    first_l.start()
 
     loads[2].wait()
     lines = f_raw[...].astype(f32)
@@ -189,6 +187,8 @@
         return 0
 
     lax.fori_loop(0, NCH, mix, 0, unroll=2)
+    first_r.start()
+    first_l.start()
     second_r.start()
     second_l.start()
     f_all[s] = f_own[s]

time: 110 us -> 110 us (level)
  no operation moved by 1% of the time
where the time goes in v3:
time: 110 us
  Pallas kernels  110 us (100%)
    pallas_call x1, Pallas kernels, local(): pl.pallas_call(kernel, out_shape=(jax.ShapeDtypeStruct((SEQ, SUB, TOK), b...  106 us
    pallas_call x1, Pallas kernels, local(): pl.pallas_call(finish_kernel, out_shape=(stream,) * 4, grid=(WID // width...  3.1 us

profile of v3, /device:TPU:1, one launch (start us, length us, event | category | flops | bytes accessed | tf_op | source)
XLA Modules:
  0.0 110.1 jit_solution(4001906910530092095)
XLA Ops:
  0.6 106.4 %shard_map.93 = (bf16[64,16,256]{2,1,0:T(8,128)(2,1)}, bf16[256,1024]{1,0:T(8,128)(2,1)}, bf16[256,1024]{1,0:T(8,128)(2,1)}, bf16[256,1024]{1,0:T(8,128)(2,1)}, bf16[256,1024]{1,0:T(8,128)(2,1)}) custom-call(bf16[256,1024]{1,0:T(8,128)(2,1)} %q_hbm.1, bf16[256,1024]{1,0:T(8,128)(2,1)} %k.1, bf16[256,1024]{1,0:T(8,128)(2,1)} %v.1, bf16[64,256]{1,0:T(8,128)(2,1)} %f_hbm.1, ...), custom_call_target="tpu_custom_call" | custom-call | flops 17999998976 | bytes 12582912 | tf_op jit(solution)/shard_map/pallas_call | solution.py:361
  107.0 3.1 %shard_map.94 = (bf16[256,1024]{1,0:T(8,128)(2,1)}, bf16[256,1024]{1,0:T(8,128)(2,1)}, bf16[256,1024]{1,0:T(8,128)(2,1)}, bf16[256,1024]{1,0:T(8,128)(2,1)}) custom-call(bf16[64,16,256]{2,1,0:T(8,128)(2,1)} %get-tuple-element.9.gm_t, bf16[256,1024]{1,0:T(8,128)(2,1)} %k.1, bf16[256,1024]{1,0:T(8,128)(2,1)} %v.1, bf16[256,1024]{1,0:T(8,128)(2,1)} %get-tuple-element.10.qg_in, ...), custom_call_target="tpu_custom_call" | custom-call | flops 4000000 | bytes 6291456 | tf_op jit(solution)/shard_map/pallas_call | solution.py:396
